TPU v7x, 32 devices: a whole 2x2x4 slice. The times are simulated.
32 devices in a mesh: clips: 2 (over x), frames: 2 (over core), rows: 8 (over z, y).
Axes of the slice: x: 2, y: 2, z: 4, core: 2. Of those that a mesh axis runs over, the one named last changes fastest.
Arguments:
- noisy_video: bfloat16 [4, 64, 1024, 128], P(('clips', 'frames'), 'rows'), parts along dimension 0, may hold values from -60 to 60
- timestep: int32 [2], P('clips'), parts along dimension 0, may hold values from 100 to 899
- embed_weight: bfloat16 [512, 256], replicated, may hold values from -0.25 to 0.25
- norm_gain: float32 [2, 128], replicated, may hold values from 0.1 to 1.9
- norm_bias: float32 [2, 128], replicated, may hold values from -2.4 to 2.4
- conv_first: bfloat16 [3, 3, 128, 128], replicated, may hold values from -0.1875 to 0.1875
- temporal_weight: bfloat16 [3, 128, 128], replicated, may hold values from -0.3125 to 0.3125
- conv_second: bfloat16 [3, 3, 128, 128], replicated, may hold values from -0.1875 to 0.1875
Outputs:
- next_video: bfloat16 [4, 64, 1024, 128], P(('clips', 'frames'), 'rows'), parts along dimension 0
- predicted: float32 [4, 64, 1024, 128], P(('clips', 'frames'), 'rows'), parts along dimension 0
There are 2 independent parts, one for each index of `clips`. A program takes and returns all parts, laid end to end along the dimension named above; an argument that names none is the same for every part. Nothing has to cross between parts.
All inputs are finite; a program needn't handle non-finite values.
Results may differ from a plain program's by a relative error of at most 0.002.
Values may be sent and summed in bfloat16 or wider, within the bound.
A program may use at most 128 MiB of HBM per device.

v0:
```python
import math

import jax
import jax.numpy as jnp
from jax import lax
from jax.sharding import PartitionSpec as P

GROUPS = 32
TSTEPS = 1000
STRIDE = 8


def extended_2(block, sides, width):
    for axis, dim in sides:
        count = lax.axis_size(axis)
        forward = [(i, i + 1) for i in range(count - 1)]
        backward = [(target, source) for source, target in forward]
        low = lax.ppermute(
            lax.slice_in_dim(block, block.shape[dim] - width, None, axis=dim), axis, forward
        )
        high = lax.ppermute(lax.slice_in_dim(block, 0, width, axis=dim), axis, backward)
        block = jnp.concatenate([low, block, high], axis=dim)
    return block


def signal_noise(step_value):
    frac = (step_value.astype(jnp.float32) / TSTEPS + 0.008) / 1.008
    level = jnp.cos(frac * (math.pi / 2)) ** 2
    return (jnp.sqrt(level), jnp.sqrt(1.0 - level))


def embed_time(step_value, embed_weight):
    half = embed_weight.shape[0] // 2
    freqs = jnp.exp(-math.log(10000.0) * jnp.arange(half, dtype=jnp.float32) / half)
    angles = step_value.astype(jnp.float32) * freqs
    feats = jnp.concatenate([jnp.sin(angles), jnp.cos(angles)]).astype(jnp.bfloat16)
    film = jnp.dot(feats[None, :], embed_weight, preferred_element_type=jnp.float32)[0]
    channels = embed_weight.shape[1] // 2
    return (film[:channels], film[channels:])


def norm_factors(values):
    frames, height, width, channels = values.shape
    groups = GROUPS
    grouped = values.reshape(frames, height, width, groups, channels // groups)
    first = jnp.sum(grouped, axis=(1, 2, 4))
    second = jnp.sum(grouped * grouped, axis=(1, 2, 4))
    first, second = lax.psum((first, second), "rows")
    count = height * lax.axis_size("rows") * width * (channels // groups)
    mean = first / count
    inverse = lax.rsqrt(second / count - mean * mean + 1e-05)
    mean_ch = jnp.repeat(mean, channels // groups, axis=1)[:, None, None, :]
    inv_ch = jnp.repeat(inverse, channels // groups, axis=1)[:, None, None, :]
    return (mean_ch, inv_ch)


def spatial_conv(extended, kernel):
    padded = jnp.pad(extended, ((0, 0), (0, 0), (1, 1), (0, 0)))
    height = extended.shape[1] - 2
    width = extended.shape[2]
    total = None
    for offset_row in range(3):
        for offset_col in range(3):
            window = padded[:, offset_row : offset_row + height, offset_col : offset_col + width, :]
            term = jnp.einsum(
                "frwc,cd->frwd",
                window,
                kernel[offset_row, offset_col],
                preferred_element_type=jnp.float32,
            )
            total = term if total is None else total + term
    return total


def temporal_conv(framed, temporal_weight):
    frames = framed.shape[0] - 2
    total = None
    for offset in range(3):
        term = jnp.einsum(
            "frwc,cd->frwd",
            framed[offset : offset + frames],
            temporal_weight[offset],
            preferred_element_type=jnp.float32,
        )
        total = term if total is None else total + term
    return total.astype(jnp.bfloat16)


def body(
    noisy_video,
    timestep,
    embed_weight,
    norm_gain,
    norm_bias,
    conv_first,
    temporal_weight,
    conv_second,
):
    step_now = timestep[0]
    scale, shift = embed_time(step_now, embed_weight)
    signal_now, noise_now = signal_noise(step_now)
    signal_prev, noise_prev = signal_noise(step_now - STRIDE)
    video = noisy_video.astype(jnp.float32)
    mean_one, inv_one = norm_factors(video)
    activated = jax.nn.silu((video - mean_one) * inv_one * norm_gain[0] + norm_bias[0]).astype(
        jnp.bfloat16
    )
    extended = extended_2(activated, (("rows", 1),), 1)
    first = (spatial_conv(extended, conv_first) * (1.0 + scale) + shift).astype(jnp.bfloat16)
    first_float = first.astype(jnp.float32)
    mean_two, inv_two = norm_factors(first_float)
    mixed = jax.nn.silu((first_float - mean_two) * inv_two * norm_gain[1] + norm_bias[1]).astype(
        jnp.bfloat16
    )
    framed = extended_2(mixed, (("frames", 0),), 1)
    temporal = temporal_conv(framed, temporal_weight)
    temporal_ext = extended_2(temporal, (("rows", 1),), 1)
    predicted = (video + spatial_conv(temporal_ext, conv_second)) * (1.0 / math.sqrt(2.0))
    estimate = (video - noise_now * predicted) / signal_now
    return ((signal_prev * estimate + noise_prev * predicted).astype(jnp.bfloat16), predicted)


def solution(mesh):
    in_specs = (
        P(("clips", "frames"), "rows", None, None),
        P("clips"),
        P(),
        P(),
        P(),
        P(),
        P(),
        P(),
    )
    out_specs = (
        P(("clips", "frames"), "rows", None, None),
        P(("clips", "frames"), "rows", None, None),
    )
    return jax.shard_map(body, mesh=mesh, in_specs=in_specs, out_specs=out_specs, check_vma=False)
```

profile of v0, /device:TPU:9, one launch (start us, length us, event | category | flops | bytes accessed | tf_op | source)
XLA Modules:
  0.0 153.6 jit_solution(1523420947911646536)
XLA Ops:
  0.7 2.7 %convert_reduce_fusion = (f32[128]{0:T(128)S(1)}, f32[128]{0:T(128)S(1)}) fusion(bf16[1,8,1024,128]{3,2,1,0:T(8,128)(2,1)} %param.8), kind=kLoop, calls=%fused_computation.4 | loop fusion | flops 4194048 | bytes 2098176 | tf_op jit(solution)/shard_map/reduce_sum | solution.py:46
  3.8 15.1 %all-reduce.3 = (f32[1,32]{1,0:T(1,128)S(1)}, f32[1,32]{1,0:T(1,128)S(1)}) all-reduce(f32[1,32]{1,0:T(1,128)S(1)} %bitcast.214, f32[1,32]{1,0:T(1,128)S(1)} %bitcast.212), channel_id=1, replica_groups=mesh['clips'=2,'frames'=2,'rows'=8] {'rows'}, use_global_device_ids=true, to_apply=%region_5.6 | all-reduce | flops 64 | bytes 512 | tf_op jit(solution)/shard_map/psum | solution.py:48
  20.1 3.1 %fusion.19 = bf16[1,8,1024,128]{3,2,1,0:T(8,128)(2,1)S(1)} fusion(bf16[1,8,1024,128]{3,2,1,0:T(8,128)(2,1)} %param.8, f32[128]{0:T(128)S(1)} %get-tuple-element.19, f32[128]{0:T(128)S(1)} %get-tuple-element.29, f32[128]{0:T(128)S(1)} %broadcast_in_dim.26, f32[128]{0:T(128)S(1)} %broadcast_in_dim.24), kind=kLoop, calls=%fused_computation.29 | loop fusion | flops 10485760 | bytes 4196352 | tf_op jit(solution)/shard_map/convert_element_type | solution.py:105
  25.2 4.3 %collective-permute-start.1 = (bf16[1,1,1024,128]{3,2,1,0:T(8,128)(2,1)S(1)}, bf16[1,1,1024,128]{3,2,1,0:T(8,128)(2,1)S(1)}, u32[]{:S(2)}, u32[]{:S(2)}) collective-permute-start(bf16[1,1,1024,128]{3,2,1,0:T(8,128)(2,1)S(1)} %get-tuple-element.15), channel_id=1, source_target_pairs={{1,0},{2,1},{3,2},{4,3},{5,4},{6,5},{7,6},{9,8},{10,9},{11,10},{12... | collective-permute-start | bytes 786440 | tf_op jit(solution)/shard_map/ppermute | solution.py:21
  31.4 6.4 %collective-permute-done.1 = bf16[1,1,1024,128]{3,2,1,0:T(8,128)(2,1)S(1)} collective-permute-done((bf16[1,1,1024,128]{3,2,1,0:T(8,128)(2,1)S(1)}, bf16[1,1,1024,128]{3,2,1,0:T(8,128)(2,1)S(1)}, u32[]{:S(2)}, u32[]{:S(2)}) %collective-permute-start.1) | collective-permute-done | bytes 262176 | tf_op jit(solution)/shard_map/ppermute | solution.py:21
  39.8 2.6 %fusion.50 = f32[8,1024,128]{2,1,0:T(8,128)} fusion(bf16[1,10,1026,128]{3,2,1,0:T(8,128)(2,1)S(1)} %fusion.29, bf16[3,3,128,128]{3,2,1,0:T(8,128)(2,1)S(1)} %copy-done.5), kind=kOutput, calls=%fused_computation.73 | convolution fusion | flops 268435456 | bytes 6324224 | tf_op jit(solution)/shard_map/frwc,cd->frwd/dot_general | solution.py:65
  42.4 2.7 %fusion.51 = f32[8,1024,128]{2,1,0:T(8,128)} fusion(bf16[1,10,1026,128]{3,2,1,0:T(8,128)(2,1)S(1)} %fusion.29, bf16[3,3,128,128]{3,2,1,0:T(8,128)(2,1)S(1)} %copy-done.5), kind=kOutput, calls=%fused_computation.75 | convolution fusion | flops 268435456 | bytes 6324224 | tf_op jit(solution)/shard_map/frwc,cd->frwd/dot_general | solution.py:65
  45.1 2.7 %fusion.52 = f32[8,1024,128]{2,1,0:T(8,128)} fusion(bf16[1,10,1026,128]{3,2,1,0:T(8,128)(2,1)S(1)} %fusion.29, bf16[3,3,128,128]{3,2,1,0:T(8,128)(2,1)S(1)} %copy-done.5), kind=kOutput, calls=%fused_computation.77 | convolution fusion | flops 268435456 | bytes 6324224 | tf_op jit(solution)/shard_map/frwc,cd->frwd/dot_general | solution.py:65
  47.8 2.7 %fusion.57 = f32[8,1024,128]{2,1,0:T(8,128)} fusion(bf16[1,10,1026,128]{3,2,1,0:T(8,128)(2,1)S(1)} %fusion.29, bf16[3,3,128,128]{3,2,1,0:T(8,128)(2,1)S(1)} %copy-done.5), kind=kOutput, calls=%fused_computation.83 | convolution fusion | flops 268435456 | bytes 6324224 | tf_op jit(solution)/shard_map/frwc,cd->frwd/dot_general | solution.py:65
  50.4 2.7 %fusion.46 = f32[8,1024,128]{2,1,0:T(8,128)} fusion(bf16[1,1,1024,128]{3,2,1,0:T(8,128)(2,1)S(1)} %collective-permute-done.1, bf16[1,8,1024,128]{3,2,1,0:T(8,128)(2,1)S(1)} %fusion.19, bf16[3,3,128,128]{3,2,1,0:T(8,128)(2,1)S(1)} %copy-done.5), kind=kOutput, calls=%fused_computation.68 | convolution fusion | flops 269484032 | bytes 6586368 | tf_op jit(solution)/shard_map/frwc,cd->frwd/dot_general | solution.py:65
  55.8 11.0 %convert_reduce_fusion.1 = (f32[128]{0:T(128)S(1)}, f32[128]{0:T(128)S(1)}, bf16[8,1024,128]{2,1,0:T(8,128)(2,1)}) fusion(f32[128]{0:T(128)S(1)} %get-tuple-element.21, f32[128]{0:T(128)S(1)} %get-tuple-element.20, bf16[3,3,128,128]{3,2,1,0:T(8,128)(2,1)S(1)} %copy-done.5, bf16[1,10,1026,128]{3,2,1,0:T(8,128)(2,1)S(1)} %fusion.29, ...), kind=kOutput, calls=%fused_computation.9 | convolution fusion | flops 284163840 | bytes 37783552 | tf_op jit(solution)/shard_map/frwc,cd->frwd/dot_general | solution.py:65
  67.3 11.8 %all-reduce.2 = (f32[1,32]{1,0:T(1,128)S(1)}, f32[1,32]{1,0:T(1,128)S(1)}) all-reduce(f32[1,32]{1,0:T(1,128)S(1)} %bitcast.213, f32[1,32]{1,0:T(1,128)S(1)} %bitcast.211), channel_id=1, replica_groups=mesh['clips'=2,'frames'=2,'rows'=8] {'rows'}, use_global_device_ids=true, to_apply=%region_11.12 | all-reduce | flops 64 | bytes 512 | tf_op jit(solution)/shard_map/psum | solution.py:48
  79.5 4.4 %fusion.121 = bf16[1,8,1024,128]{3,2,1,0:T(8,128)(2,1)} fusion(f32[128]{0:T(128)S(1)} %get-tuple-element.18, f32[128]{0:T(128)S(1)} %get-tuple-element.30, f32[128]{0:T(128)S(1)} %broadcast_in_dim.30, f32[128]{0:T(128)S(1)} %broadcast_in_dim.28, bf16[8,1024,128]{2,1,0:T(8,128)(2,1)} %get-tuple-element.26), kind=kLoop, calls=%fused_computation.155 | loop fusion | flops 10485760 | bytes 4196352 | tf_op jit(solution)/shard_map/convert_element_type | solution.py:112
  85.2 11.6 %collective-permute-start.3 = (bf16[1,8,1024,128]{3,2,1,0:T(8,128)(2,1)}, bf16[1,8,1024,128]{3,2,1,0:T(8,128)(2,1)}, u32[]{:S(2)}, u32[]{:S(2)}) collective-permute-start(bf16[1,8,1024,128]{3,2,1,0:T(8,128)(2,1)} %fusion.121), channel_id=1, source_target_pairs={{8,0},{9,1},{10,2},{11,3},{12,4},{13,5},{14,6},{15,7},{24,16},{25,... | collective-permute-start | bytes 6291464 | tf_op jit(solution)/shard_map/ppermute | solution.py:21
  105.3 4.3 %collective-permute-start.5 = (bf16[1,1,1024,128]{3,2,1,0:T(8,128)(2,1)S(1)}, bf16[1,1,1024,128]{3,2,1,0:T(8,128)(2,1)S(1)}, u32[]{:S(2)}, u32[]{:S(2)}) collective-permute-start(bf16[1,1,1024,128]{3,2,1,0:T(8,128)(2,1)S(1)} %get-tuple-element.13), channel_id=1, source_target_pairs={{1,0},{2,1},{3,2},{4,3},{5,4},{6,5},{7,6},{9,8},{10,9},{11,10},{12... | collective-permute-start | bytes 786440 | tf_op jit(solution)/shard_map/ppermute | solution.py:21
  110.3 5.8 %collective-permute-done.4 = bf16[1,1,1024,128]{3,2,1,0:T(8,128)(2,1)S(1)} collective-permute-done((bf16[1,1,1024,128]{3,2,1,0:T(8,128)(2,1)S(1)}, bf16[1,1,1024,128]{3,2,1,0:T(8,128)(2,1)S(1)}, u32[]{:S(2)}, u32[]{:S(2)}) %collective-permute-start.4) | collective-permute-done | bytes 262176 | tf_op jit(solution)/shard_map/ppermute | solution.py:18
  116.2 3.3 %collective-permute-done.5 = bf16[1,1,1024,128]{3,2,1,0:T(8,128)(2,1)S(1)} collective-permute-done((bf16[1,1,1024,128]{3,2,1,0:T(8,128)(2,1)S(1)}, bf16[1,1,1024,128]{3,2,1,0:T(8,128)(2,1)S(1)}, u32[]{:S(2)}, u32[]{:S(2)}) %collective-permute-start.5) | collective-permute-done | bytes 262176 | tf_op jit(solution)/shard_map/ppermute | solution.py:21
  120.8 2.6 %fusion.35 = f32[8,1024,128]{2,1,0:T(8,128)} fusion(bf16[1,10,1026,128]{3,2,1,0:T(8,128)(2,1)S(1)} %select_maximum_fusion, bf16[3,3,128,128]{3,2,1,0:T(8,128)(2,1)S(1)} %copy-done.4), kind=kOutput, calls=%fused_computation.51 | convolution fusion | flops 268435456 | bytes 6324224 | tf_op jit(solution)/shard_map/frwc,cd->frwd/dot_general | solution.py:65
  123.5 2.7 %fusion.36 = f32[8,1024,128]{2,1,0:T(8,128)} fusion(bf16[1,10,1026,128]{3,2,1,0:T(8,128)(2,1)S(1)} %select_maximum_fusion, bf16[3,3,128,128]{3,2,1,0:T(8,128)(2,1)S(1)} %copy-done.4), kind=kOutput, calls=%fused_computation.53 | convolution fusion | flops 268435456 | bytes 6324224 | tf_op jit(solution)/shard_map/frwc,cd->frwd/dot_general | solution.py:65
  126.1 2.7 %fusion.37 = f32[8,1024,128]{2,1,0:T(8,128)} fusion(bf16[1,10,1026,128]{3,2,1,0:T(8,128)(2,1)S(1)} %select_maximum_fusion, bf16[3,3,128,128]{3,2,1,0:T(8,128)(2,1)S(1)} %copy-done.4), kind=kOutput, calls=%fused_computation.55 | convolution fusion | flops 268435456 | bytes 6324224 | tf_op jit(solution)/shard_map/frwc,cd->frwd/dot_general | solution.py:65
  128.8 2.7 %fusion.38 = f32[8,1024,128]{2,1,0:T(8,128)} fusion(bf16[1,10,1026,128]{3,2,1,0:T(8,128)(2,1)S(1)} %select_maximum_fusion, bf16[3,3,128,128]{3,2,1,0:T(8,128)(2,1)S(1)} %copy-done.4), kind=kOutput, calls=%fused_computation.57 | convolution fusion | flops 268435456 | bytes 6324224 | tf_op jit(solution)/shard_map/frwc,cd->frwd/dot_general | solution.py:65
  134.1 2.7 %fusion.40 = f32[8,1024,128]{2,1,0:T(8,128)} fusion(bf16[1,8,1024,128]{3,2,1,0:T(8,128)(2,1)S(1)} %bitcast.208, bf16[1,1,1024,128]{3,2,1,0:T(8,128)(2,1)S(1)} %collective-permute-done.4, bf16[3,3,128,128]{3,2,1,0:T(8,128)(2,1)S(1)} %copy-done.4), kind=kOutput, calls=%fused_computation.60 | convolution fusion | flops 269484032 | bytes 6586368 | tf_op jit(solution)/shard_map/frwc,cd->frwd/dot_general | solution.py:65
  136.7 2.7 %fusion.32 = f32[8,1024,128]{2,1,0:T(8,128)} fusion(bf16[1,1,1024,128]{3,2,1,0:T(8,128)(2,1)S(1)} %collective-permute-done.5, bf16[1,8,1024,128]{3,2,1,0:T(8,128)(2,1)S(1)} %bitcast.209, bf16[3,3,128,128]{3,2,1,0:T(8,128)(2,1)S(1)} %copy-done.4), kind=kOutput, calls=%fused_computation.48 | convolution fusion | flops 269484032 | bytes 6586368 | tf_op jit(solution)/shard_map/frwc,cd->frwd/dot_general | solution.py:65
  139.5 14.0 %broadcast_multiply_fusion = (f32[1,8,1024,128]{3,2,1,0:T(8,128)}, bf16[1,8,1024,128]{3,2,1,0:T(8,128)(2,1)}) fusion(f32[]{:T(128)} %bitcast.79, f32[]{:T(128)S(6)} %sqrt.14, f32[]{:T(128)S(6)} %mul.139, bf16[1,8,1024,128]{3,2,1,0:T(8,128)(2,1)S(1)} %copy-done.2, f32[]{:T(128)} %bitcast, bf16[3,3,128,128]{3,2,1,0:T(8,128)(2,1)S(1)} %copy-done.4, ...), kind=kOutput, calls=%fused_computation.90 | convolution fusion | flops 287309824 | bytes 44072976 | tf_op jit(solution)/shard_map/frwc,cd->frwd/dot_general | solution.py:65
  (56 shorter events, 24.3 us)
Async XLA Ops:
  0.6 30.2 %copy-start = (bf16[512,256]{1,0:T(8,128)(2,1)S(1)}, bf16[512,256]{1,0:T(8,128)(2,1)}, u32[]{:S(2)}) copy-start(bf16[512,256]{1,0:T(8,128)(2,1)} %param.10) | copy-start | bytes 786436
  0.6 28.8 %copy-start.5 = (bf16[3,3,128,128]{3,2,1,0:T(8,128)(2,1)S(1)}, bf16[3,3,128,128]{3,2,1,0:T(8,128)(2,1)}, u32[]{:S(2)}) copy-start(bf16[3,3,128,128]{3,2,1,0:T(8,128)(2,1)} %param.13) | copy-start | bytes 884740
  23.2 8.1 %collective-permute-start = (bf16[1,1,1024,128]{3,2,1,0:T(8,128)(2,1)S(1)}, bf16[1,1,1024,128]{3,2,1,0:T(8,128)(2,1)S(1)}, u32[]{:S(2)}, u32[]{:S(2)}) collective-permute-start(bf16[1,1,1024,128]{3,2,1,0:T(8,128)(2,1)S(1)} %get-tuple-element.14), channel_id=1, source_target_pairs={{0,1},{1,2},{2,3},{3,4},{4,5},{5,6},{6,7},{8,9},{9,10},{10,11},{11... | collective-permute-start | bytes 786440 | tf_op jit(solution)/shard_map/ppermute | solution.py:18
  25.2 12.6 %collective-permute-start.1 = (bf16[1,1,1024,128]{3,2,1,0:T(8,128)(2,1)S(1)}, bf16[1,1,1024,128]{3,2,1,0:T(8,128)(2,1)S(1)}, u32[]{:S(2)}, u32[]{:S(2)}) collective-permute-start(bf16[1,1,1024,128]{3,2,1,0:T(8,128)(2,1)S(1)} %get-tuple-element.15), channel_id=1, source_target_pairs={{1,0},{2,1},{3,2},{4,3},{5,4},{6,5},{7,6},{9,8},{10,9},{11,10},{12... | collective-permute-start | bytes 786440 | tf_op jit(solution)/shard_map/ppermute | solution.py:21
  66.8 30.3 %copy-start.3 = (bf16[8,1024,128]{2,1,0:T(8,128)(2,1)S(1)}, bf16[8,1024,128]{2,1,0:T(8,128)(2,1)}, u32[]{:S(2)}) copy-start(bf16[8,1024,128]{2,1,0:T(8,128)(2,1)} %get-tuple-element.26) | copy-start | bytes 6291460
  66.8 30.3 %copy-start.6 = (bf16[3,128,128]{2,1,0:T(8,128)(2,1)S(1)}, bf16[3,128,128]{2,1,0:T(8,128)(2,1)}, u32[]{:S(2)}) copy-start(bf16[3,128,128]{2,1,0:T(8,128)(2,1)} %param.14) | copy-start | bytes 294916
  83.9 14.8 %collective-permute-start.2 = (bf16[1,8,1024,128]{3,2,1,0:T(8,128)(2,1)}, bf16[1,8,1024,128]{3,2,1,0:T(8,128)(2,1)}, u32[]{:S(2)}, u32[]{:S(2)}) collective-permute-start(bf16[1,8,1024,128]{3,2,1,0:T(8,128)(2,1)} %fusion.121), channel_id=1, source_target_pairs={{0,8},{1,9},{2,10},{3,11},{4,12},{5,13},{6,14},{7,15},{16,24},{17,... | collective-permute-start | bytes 6291464 | tf_op jit(solution)/shard_map/ppermute | solution.py:18
  85.2 15.9 %collective-permute-start.3 = (bf16[1,8,1024,128]{3,2,1,0:T(8,128)(2,1)}, bf16[1,8,1024,128]{3,2,1,0:T(8,128)(2,1)}, u32[]{:S(2)}, u32[]{:S(2)}) collective-permute-start(bf16[1,8,1024,128]{3,2,1,0:T(8,128)(2,1)} %fusion.121), channel_id=1, source_target_pairs={{8,0},{9,1},{10,2},{11,3},{12,4},{13,5},{14,6},{15,7},{24,16},{25,... | collective-permute-start | bytes 6291464 | tf_op jit(solution)/shard_map/ppermute | solution.py:21
  101.0 8.6 %copy-start.4 = (bf16[3,3,128,128]{3,2,1,0:T(8,128)(2,1)S(1)}, bf16[3,3,128,128]{3,2,1,0:T(8,128)(2,1)}, u32[]{:S(2)}) copy-start(bf16[3,3,128,128]{3,2,1,0:T(8,128)(2,1)} %param.15) | copy-start | bytes 884740
  103.4 12.7 %collective-permute-start.4 = (bf16[1,1,1024,128]{3,2,1,0:T(8,128)(2,1)S(1)}, bf16[1,1,1024,128]{3,2,1,0:T(8,128)(2,1)S(1)}, u32[]{:S(2)}, u32[]{:S(2)}) collective-permute-start(bf16[1,1,1024,128]{3,2,1,0:T(8,128)(2,1)S(1)} %get-tuple-element.12), channel_id=1, source_target_pairs={{0,1},{1,2},{2,3},{3,4},{4,5},{5,6},{6,7},{8,9},{9,10},{10,11},{11... | collective-permute-start | bytes 786440 | tf_op jit(solution)/shard_map/ppermute | solution.py:18
  105.3 14.1 %collective-permute-start.5 = (bf16[1,1,1024,128]{3,2,1,0:T(8,128)(2,1)S(1)}, bf16[1,1,1024,128]{3,2,1,0:T(8,128)(2,1)S(1)}, u32[]{:S(2)}, u32[]{:S(2)}) collective-permute-start(bf16[1,1,1024,128]{3,2,1,0:T(8,128)(2,1)S(1)} %get-tuple-element.13), channel_id=1, source_target_pairs={{1,0},{2,1},{3,2},{4,3},{5,4},{6,5},{7,6},{9,8},{10,9},{11,10},{12... | collective-permute-start | bytes 786440 | tf_op jit(solution)/shard_map/ppermute | solution.py:21
  136.7 2.7 %copy-start.2 = (bf16[1,8,1024,128]{3,2,1,0:T(8,128)(2,1)S(1)}, bf16[1,8,1024,128]{3,2,1,0:T(8,128)(2,1)}, u32[]{:S(2)}) copy-start(bf16[1,8,1024,128]{3,2,1,0:T(8,128)(2,1)} %param.8) | copy-start | bytes 6291460
  139.4 14.0 %copy-start.1 = (bf16[512,256]{1,0:T(8,128)(2,1)S(1)}, bf16[512,256]{1,0:T(8,128)(2,1)}, u32[]{:S(2)}) copy-start(bf16[512,256]{1,0:T(8,128)(2,1)} %param.10) | copy-start | bytes 786436
where the time goes:
time: 154 us
  matrix products  68 us (44%)
  blocking collectives  26.9 us (17%)
  starting transfers between devices  25.3 us (16%)
  waiting for transfers between devices  15.8 us (10%)
  other arithmetic  13.5 us (9%)
  between operations  2.05 us (1%)
  local copies, waits for them, and re-layouts  1.99 us (1%)
    dot_general x18, matrix products, spatial_conv(): jnp.einsum('frwc,cd->frwd', window, kernel[offset_row, offset_col], prefe...  61.7 us
    psum x2, blocking collectives, norm_factors(): first, second = lax.psum((first, second), 'rows')  26.9 us
    ppermute x3, starting transfers between devices, extended_2(): lax.ppermute(lax.slice_in_dim(block, 0, width, axis=dim), axis, backward)  20.2 us
    ppermute x3, waiting for transfers between devices, extended_2(): lax.ppermute(lax.slice_in_dim(block, 0, width, axis=dim), axis, backward)  9.68 us
    dot_general x3, matrix products, temporal_conv(): jnp.einsum('frwc,cd->frwd', framed[offset:offset + frames], temporal_weig...  6.17 us
    ppermute x3, waiting for transfers between devices, extended_2(): lax.ppermute(lax.slice_in_dim(block, block.shape[dim] - width, None, axis...  6.17 us
    ppermute x3, starting transfers between devices, extended_2(): lax.ppermute(lax.slice_in_dim(block, block.shape[dim] - width, None, axis...  5.12 us
    convert_element_type x1, other arithmetic, body(): jax.nn.silu((first_float - mean_two) * inv_two * norm_gain[1] + norm_bias...  4.41 us
  transfers between devices with their start and end apart: 6, of which 4 were waited for; matrix products, arithmetic and copies ran while one was open for 4% of the time, Pallas kernels for 0%

commit v1 on v0

v1 whole, which is shorter than its diff:
```python
import functools
import math

import jax
import jax.numpy as jnp
import numpy as np
from jax import lax
from jax.experimental import pallas as pl
from jax.experimental.pallas import tpu as pltpu
from jax.sharding import PartitionSpec as P

GROUPS = 32
TSTEPS = 1000
STRIDE = 8
F32 = jnp.float32
BF16 = jnp.bfloat16
MESH = pl.DeviceIdType.MESH


def signal_noise(step_value):
    frac = (step_value / TSTEPS + 0.008) / 1.008
    level = jnp.cos(frac * (math.pi / 2)) ** 2
    return (jnp.sqrt(level), jnp.sqrt(1.0 - level))


def half_factors(stat, count, gain, bias):
    channels = stat.shape[1]
    size = channels // GROUPS
    row = lax.broadcasted_iota(jnp.int32, (channels, channels), 0) // size
    col = lax.broadcasted_iota(jnp.int32, (channels, channels), 1) // size
    same = jnp.where(row == col, 1.0, 0.0).astype(F32)
    sums = jnp.dot(stat, same, precision=lax.Precision.HIGHEST, preferred_element_type=F32)
    mean = sums[0:1] / count
    inverse = lax.rsqrt(sums[1:2] / count - mean * mean + 1e-05)
    a = inverse * gain
    return 0.5 * a, 0.5 * (bias - mean * a)


def half_silu(h):
    return h + h * jnp.tanh(h)


def put_taps(dst_ref, row, value):
    width, channels = value.shape
    pos = lax.broadcasted_iota(jnp.int32, value.shape, 0)
    left = jnp.where(pos == 0, 0.0, pltpu.roll(value, 1, 0))
    right = jnp.where(pos == width - 1, 0.0, pltpu.roll(value, width - 1, 0))
    dst_ref[row, :, 0:channels] = left.astype(BF16)
    dst_ref[row, :, channels : 2 * channels] = value.astype(BF16)
    dst_ref[row, :, 2 * channels : 3 * channels] = right.astype(BF16)


def put_weights(wide_ref, w_ref):
    channels = w_ref.shape[-1]
    for i in range(4):
        for o in range(2):
            for b in range(3):
                k = (i * 3 + b) * channels
                tap = i - o
                block = (
                    w_ref[tap, b]
                    if 0 <= tap <= 2
                    else jnp.zeros((channels, channels), BF16)
                )
                wide_ref[k : k + channels, o * channels : (o + 1) * channels] = block


def pair_dot(taps_ref, base, cols, wide_ref):
    lhs = jnp.concatenate([taps_ref[base + i, cols, :] for i in range(4)], axis=1)
    return jnp.dot(lhs, wide_ref[...], preferred_element_type=F32)


def fold8(x):
    return jnp.sum(x.reshape(x.shape[0] // 8, 8, x.shape[1]), axis=0)


def front(
    n,
    t_ref,
    video_ref,
    freqs_ref,
    embed_ref,
    gain_ref,
    bias_ref,
    w_ref,
    firsts_ref,
    stat_ref,
    halo,
    act,
    wide,
    first,
    s1_send,
    s1_recv,
    s2_send,
    s2_recv,
    sums,
    halo_ss,
    halo_rs,
    s1_ss,
    s1_rs,
    s2_ss,
    s2_rs,
    core_ss,
    core_rs,
    edge_ss,
    edge_rs,
    own_sem,
):
    height, width, channels = video_ref.shape
    pairs = height // 2
    f = lax.axis_index("frames")
    r = lax.axis_index("rows")
    me = f * n + r
    barrier = pltpu.get_barrier_semaphore()

    def peer(d):
        q = lax.rem(me + d, 2 * n)
        return q, {"frames": q // n, "rows": lax.rem(q, n)}

    @pl.loop(1, 2 * n)
    def _(d):
        _, device = peer(d)
        pl.semaphore_signal(barrier, 1, device_id=device, device_id_type=MESH)

    sums[...] = jnp.zeros_like(sums)

    @pl.loop(0, height)
    def _(h):
        x = video_ref[h].astype(F32)
        sums[0] += fold8(x)
        sums[1] += fold8(x * x)

    s1_send[...] = jnp.zeros_like(s1_send)
    s1_send[0:1] = jnp.sum(sums[0], axis=0, keepdims=True)
    s1_send[1:2] = jnp.sum(sums[1], axis=0, keepdims=True)
    s1_recv[r] = s1_send[...]
    pl.semaphore_wait(barrier, 2 * n - 1)

    def s1_copy(src_row, dst_row):
        return pltpu.make_async_remote_copy(
            s1_send,
            s1_recv.at[src_row],
            s1_ss.at[dst_row],
            s1_rs.at[src_row],
            device_id={"frames": f, "rows": dst_row},
            device_id_type=MESH,
        )

    @pl.loop(1, n)
    def _(d):
        s1_copy(r, lax.rem(r + d, n)).start()

    def halo_copy(side, target):
        return pltpu.make_async_remote_copy(
            video_ref.at[height - 1 if side == 0 else 0],
            halo.at[side],
            halo_ss.at[side],
            halo_rs.at[side],
            device_id={"frames": f, "rows": target},
            device_id_type=MESH,
        )

    has_low = r > 0
    has_high = r < n - 1

    @pl.when(has_high)
    def _():
        halo_copy(0, r + 1).start()

    @pl.when(has_low)
    def _():
        halo_copy(1, r - 1).start()

    put_weights(wide, w_ref)
    angles = t_ref[0].astype(F32) * jnp.broadcast_to(freqs_ref[...], (16, freqs_ref.shape[1]))
    feats = jnp.concatenate([jnp.sin(angles), jnp.cos(angles)], axis=1).astype(BF16)
    film = jnp.dot(feats, embed_ref[...], preferred_element_type=F32)[0:1]
    scale = 1.0 + film[:, :channels]
    shift = film[:, channels:]

    @pl.loop(1, n)
    def _(d):
        q = lax.rem(r + d, n)
        s1_copy(q, q).wait_recv()

    count = float(height * n * width * (channels // GROUPS))
    a, b = half_factors(jnp.sum(s1_recv[...], axis=0), count, gain_ref[0:1], bias_ref[0:1])

    def activate(x, row):
        h = x.astype(F32) * a + b
        put_taps(act, row, half_silu(h).astype(BF16).astype(F32))

    @pl.loop(0, height)
    def _(h):
        activate(video_ref[h], h + 1)

    zeros = jnp.zeros((width, 3 * channels), BF16)

    @pl.when(has_low)
    def _():
        halo_copy(0, r - 1).wait_recv()
        activate(halo[0], 0)

    @pl.when(r == 0)
    def _():
        act[0] = zeros

    @pl.when(has_high)
    def _():
        halo_copy(1, r + 1).wait_recv()
        activate(halo[1], height + 1)

    @pl.when(r == n - 1)
    def _():
        act[height + 1] = zeros

    def core_copy(p):
        return pltpu.make_async_remote_copy(
            first.at[pl.ds(2 * p, 2)],
            firsts_ref.at[1, pl.ds(1 + 2 * p, 2)],
            core_ss.at[p],
            core_rs.at[p],
            device_id={"frames": 1 - f, "rows": r},
            device_id_type=MESH,
        )

    def own_copy(p):
        return pltpu.make_async_copy(
            first.at[pl.ds(2 * p, 2)], firsts_ref.at[0, pl.ds(1 + 2 * p, 2)], own_sem.at[p]
        )

    def edge_copy(side, other, target):
        return pltpu.make_async_remote_copy(
            first.at[height - 1 if side == 0 else 0],
            firsts_ref.at[other, 0 if side == 0 else height + 1],
            edge_ss.at[side, other],
            edge_rs.at[side, other],
            device_id={"frames": 1 - f if other else f, "rows": target},
            device_id_type=MESH,
        )

    sums[...] = jnp.zeros_like(sums)
    step = width // 2
    order = [0] + ([pairs - 1] if pairs > 1 else []) + list(range(1, pairs - 1))
    for p in order:

        @pl.loop(0, width // step)
        def _(c):
            cols = pl.ds(pl.multiple_of(c * step, step), step)
            acc = pair_dot(act, 2 * p, cols, wide)
            for o in range(2):
                out = (acc[:, o * channels : (o + 1) * channels] * scale + shift).astype(BF16)
                first[2 * p + o, cols, :] = out
                value = out.astype(F32)
                sums[0] += fold8(value)
                sums[1] += fold8(value * value)

        core_copy(p).start()
        own_copy(p).start()
        if p == 0:

            @pl.when(has_low)
            def _():
                edge_copy(1, 0, r - 1).start()
                edge_copy(1, 1, r - 1).start()

        if p == pairs - 1:

            @pl.when(has_high)
            def _():
                edge_copy(0, 0, r + 1).start()
                edge_copy(0, 1, r + 1).start()

    s2_send[...] = jnp.zeros_like(s2_send)
    s2_send[0:1] = jnp.sum(sums[0], axis=0, keepdims=True)
    s2_send[1:2] = jnp.sum(sums[1], axis=0, keepdims=True)
    s2_recv[me] = s2_send[...]

    def s2_copy(source, q, device):
        return pltpu.make_async_remote_copy(
            s2_send,
            s2_recv.at[source],
            s2_ss.at[q],
            s2_rs.at[source],
            device_id=device,
            device_id_type=MESH,
        )

    @pl.loop(1, 2 * n)
    def _(d):
        q, device = peer(d)
        s2_copy(me, q, device).start()

    @pl.loop(1, 2 * n)
    def _(d):
        q, device = peer(d)
        s2_copy(q, q, device).wait_recv()

    stat_ref[0] = jnp.sum(s2_recv[pl.ds(f * n, n)], axis=0)
    stat_ref[1] = jnp.sum(s2_recv[pl.ds((1 - f) * n, n)], axis=0)

    for p in range(pairs):
        core_copy(p).wait()
        own_copy(p).wait()

    @pl.when(has_low)
    def _():
        halo_copy(1, r - 1).wait_send()
        for other in range(2):
            edge_copy(1, other, r - 1).wait_send()
            edge_copy(0, other, r - 1).wait_recv()

    @pl.when(has_high)
    def _():
        halo_copy(0, r + 1).wait_send()
        for other in range(2):
            edge_copy(0, other, r + 1).wait_send()
            edge_copy(1, other, r + 1).wait_recv()

    @pl.loop(1, n)
    def _(d):
        s1_copy(r, lax.rem(r + d, n)).wait_send()

    @pl.loop(1, 2 * n)
    def _(d):
        q, device = peer(d)
        s2_copy(me, q, device).wait_send()


def back(
    n,
    t_ref,
    firsts_ref,
    stat_ref,
    video_ref,
    gain_ref,
    bias_ref,
    tw_ref,
    w_ref,
    next_ref,
    pred_ref,
    taps,
    wide,
    wtime,
    factors,
    *,
    height,
):
    width, channels = firsts_ref.shape[2:]
    s = pl.program_id(0)
    f = lax.axis_index("frames")
    r = lax.axis_index("rows")

    @pl.when(s == 0)
    def _():
        put_weights(wide, w_ref)
        wtime[0:channels] = tw_ref[1]
        wtime[channels : 2 * channels] = tw_ref[2 - 2 * f]
        count = float(height * n * width * (channels // GROUPS))
        for i in range(2):
            a, b = half_factors(stat_ref[i], count, gain_ref[1:2], bias_ref[1:2])
            factors[2 * i : 2 * i + 1] = a
            factors[2 * i + 1 : 2 * i + 2] = b
        step_now = jnp.full((8, channels), t_ref[0].astype(F32))
        signal_now, noise_now = signal_noise(step_now)
        signal_prev, noise_prev = signal_noise(step_now - STRIDE)
        ratio = signal_prev / signal_now
        factors[4:5] = ratio[0:1]
        factors[5:6] = (noise_prev - ratio * noise_now)[0:1]

    for j in range(2):
        row = 2 * s + j
        mixed = []
        for i in range(2):
            h = firsts_ref[i, j].astype(F32) * factors[2 * i : 2 * i + 1] + factors[
                2 * i + 1 : 2 * i + 2
            ]
            mixed.append(half_silu(h).astype(BF16))
        value = jnp.dot(
            jnp.concatenate(mixed, axis=1), wtime[...], preferred_element_type=F32
        )
        where = r * height + row - 1
        inside = jnp.logical_and(where >= 0, where < n * height)
        value = jnp.where(inside, value, 0.0)
        put_taps(taps, row, value.astype(BF16).astype(F32))

    @pl.when(s > 0)
    def _():
        step = width // 2

        @pl.loop(0, width // step)
        def _(c):
            cols = pl.ds(pl.multiple_of(c * step, step), step)
            acc = pair_dot(taps, 2 * (s - 1), cols, wide)
            for o in range(2):
                video = video_ref[o, cols, :].astype(F32)
                predicted = (video + acc[:, o * channels : (o + 1) * channels]) * (
                    1.0 / math.sqrt(2.0)
                )
                pred_ref[o, cols, :] = predicted
                next_ref[o, cols, :] = (
                    video * factors[4:5] + predicted * factors[5:6]
                ).astype(BF16)


def body(
    n,
    noisy_video,
    timestep,
    embed_weight,
    norm_gain,
    norm_bias,
    conv_first,
    temporal_weight,
    conv_second,
):
    _, height, width, channels = noisy_video.shape
    video = noisy_video[0]
    half = embed_weight.shape[0] // 2
    freqs = np.exp(
        np.float32(-math.log(10000.0)) * np.arange(half, dtype=np.float32) / np.float32(half)
    )[None, :]
    vmem = pl.BlockSpec(memory_space=pltpu.VMEM)
    smem = pl.BlockSpec(memory_space=pltpu.SMEM)
    dma = pltpu.SemaphoreType.DMA
    pairs = height // 2
    firsts, stat = pl.pallas_call(
        functools.partial(front, n),
        out_shape=(
            jax.ShapeDtypeStruct((2, height + 2, width, channels), BF16),
            jax.ShapeDtypeStruct((2, 8, channels), F32),
        ),
        in_specs=[smem] + [vmem] * 6,
        out_specs=(pl.BlockSpec(memory_space=pl.ANY), vmem),
        scratch_shapes=[
            pltpu.VMEM((2, width, channels), BF16),
            pltpu.VMEM((height + 2, width, 3 * channels), BF16),
            pltpu.VMEM((12 * channels, 2 * channels), BF16),
            pltpu.VMEM((height, width, channels), BF16),
            pltpu.VMEM((8, channels), F32),
            pltpu.VMEM((n, 8, channels), F32),
            pltpu.VMEM((8, channels), F32),
            pltpu.VMEM((2 * n, 8, channels), F32),
            pltpu.VMEM((2, 8, channels), F32),
            dma((2,)),
            dma((2,)),
            dma((n,)),
            dma((n,)),
            dma((2 * n,)),
            dma((2 * n,)),
            dma((pairs,)),
            dma((pairs,)),
            dma((2, 2)),
            dma((2, 2)),
            dma((pairs,)),
        ],
        compiler_params=pltpu.CompilerParams(
            collective_id=0, has_side_effects=True, vmem_limit_bytes=48 * 1024 * 1024
        ),
        name="front",
    )(timestep, video, jnp.asarray(freqs), embed_weight, norm_gain, norm_bias, conv_first)

    def whole(*shape):
        return pl.BlockSpec(shape, lambda s: (0,) * len(shape))

    def pair_block():
        return pl.BlockSpec((2, width, channels), lambda s: (jnp.maximum(s - 1, 0), 0, 0))

    next_video, predicted = pl.pallas_call(
        functools.partial(back, n, height=height),
        grid=(pairs + 1,),
        out_shape=(
            jax.ShapeDtypeStruct((height, width, channels), BF16),
            jax.ShapeDtypeStruct((height, width, channels), F32),
        ),
        in_specs=[
            smem,
            pl.BlockSpec((2, 2, width, channels), lambda s: (0, s, 0, 0)),
            whole(2, 8, channels),
            pair_block(),
            whole(*norm_gain.shape),
            whole(*norm_bias.shape),
            whole(*temporal_weight.shape),
            whole(*conv_second.shape),
        ],
        out_specs=(pair_block(), pair_block()),
        scratch_shapes=[
            pltpu.VMEM((height + 2, width, 3 * channels), BF16),
            pltpu.VMEM((12 * channels, 2 * channels), BF16),
            pltpu.VMEM((2 * channels, channels), BF16),
            pltpu.VMEM((8, channels), F32),
        ],
        compiler_params=pltpu.CompilerParams(vmem_limit_bytes=48 * 1024 * 1024),
        name="back",
    )(timestep, firsts, stat, video, norm_gain, norm_bias, temporal_weight, conv_second)
    return next_video[None], predicted[None]


def solution(mesh):
    bands = P(("clips", "frames"), "rows", None, None)
    in_specs = (bands, P("clips"), P(), P(), P(), P(), P(), P())
    return jax.shard_map(
        functools.partial(body, mesh.shape["rows"]),
        mesh=mesh,
        in_specs=in_specs,
        out_specs=(bands, bands),
        check_vma=False,
    )
```

time: 154 us -> 66.2 us (0.43)
  matrix products: 68 us -> 0 us
  Pallas kernels: 0 us -> 55.7 us
  blocking collectives: 26.9 us -> 0 us
  starting transfers between devices: 25.3 us -> 0 us
  waiting for transfers between devices: 15.8 us -> 0 us
  other arithmetic: 13.5 us -> 0 us
  local copies, waits for them, and re-layouts: 1.99 us -> 8.74 us
    dot_general x22 -> x0, matrix products: 68 us -> none  [the longest x18 61.7 us: spatial_conv(): jnp.einsum('frwc,cd->frwd', window, kernel[offset_row, offset_col], prefe...]
    pallas_call x0 -> x2, Pallas kernels: none -> 55.7 us  [the longest x1 44.4 us: body(): pl.pallas_call(functools.partial(front, n), out_shape=(jax.ShapeDtypeStru...]
    psum x2 -> x0, blocking collectives: 26.9 us -> none  [norm_factors(): first, second = lax.psum((first, second), 'rows')]
    ppermute x6 -> x0, starting transfers between devices: 25.3 us -> none  [the longest x3 20.2 us: extended_2(): lax.ppermute(lax.slice_in_dim(block, 0, width, axis=dim), axis, backward)]
    ppermute x6 -> x0, waiting for transfers between devices: 15.8 us -> none  [the longest x3 9.68 us: extended_2(): lax.ppermute(lax.slice_in_dim(block, 0, width, axis=dim), axis, backward)]
    unnamed x14 -> x20, local copies, waits for them, and re-layouts: 0.04 us -> 8.74 us
    convert_element_type x2 -> x0, other arithmetic: 7.5 us -> none  [the longest x1 4.41 us: body(): jax.nn.silu((first_float - mean_two) * inv_two * norm_gain[1] + norm_bias...]
    reduce_sum x5 -> x0, other arithmetic: 3.2 us -> none  [the longest x3 2.97 us: norm_factors(): first = jnp.sum(grouped, axis=(1, 2, 4))]
  transfers between devices with their start and end apart: 6 -> 0, of which waited for: 4 -> 0; matrix products, arithmetic and copies ran while one was open for 4% -> 0% of each run, Pallas kernels for 0% -> 0%
where the time goes in v1:
time: 66.2 us; the launch traced here: 65.8 us
  Pallas kernels  55.7 us (84%)
  local copies, waits for them, and re-layouts  8.74 us (13%)
  between operations  1.31 us (2%)
    pallas_call x1, Pallas kernels, body(): pl.pallas_call(functools.partial(front, n), out_shape=(jax.ShapeDtypeStru...  44.4 us
    pallas_call x1, Pallas kernels, body(): pl.pallas_call(functools.partial(back, n, height=height), grid=(pairs + 1...  11.3 us
    unnamed x20, local copies, waits for them, and re-layouts  8.74 us

profile of v1, /device:TPU:9, one launch (start us, length us, event | category | flops | bytes accessed | tf_op | source)
XLA Modules:
  0.0 65.8 jit_solution(14648099161467111455)
XLA Ops:
  1.3 0.0 copy-start
  1.3 1.6 %copy-done = bf16[1,8,1024,128]{3,2,1,0:T(8,128)(2,1)S(1)} copy-done((bf16[1,8,1024,128]{3,2,1,0:T(8,128)(2,1)S(1)}, bf16[1,8,1024,128]{3,2,1,0:T(8,128)(2,1)}, u32[]{:S(2)}) %copy-start) | copy-done | bytes 2097176
  2.9 0.0 copy-start.1
  2.9 1.0 %copy-done.1 = bf16[3,3,128,128]{3,2,1,0:T(8,128)(2,1)S(1)} copy-done((bf16[3,3,128,128]{3,2,1,0:T(8,128)(2,1)S(1)}, bf16[3,3,128,128]{3,2,1,0:T(8,128)(2,1)}, u32[]{:S(2)}) %copy-start.1) | copy-done | bytes 294936
  3.8 0.0 copy-start.3
  3.8 0.9 %copy-done.3 = bf16[512,256]{1,0:T(8,128)(2,1)S(1)} copy-done((bf16[512,256]{1,0:T(8,128)(2,1)S(1)}, bf16[512,256]{1,0:T(8,128)(2,1)}, u32[]{:S(2)}) %copy-start.3) | copy-done | bytes 262168
  4.8 0.0 copy-start.5
  4.8 0.7 %copy-done.5 = f32[2,128]{1,0:T(2,128)S(1)} copy-done((f32[2,128]{1,0:T(2,128)S(1)}, f32[2,128]{1,0:T(2,128)}, u32[]{:S(2)}) %copy-start.5) | copy-done | bytes 1048
  5.5 0.0 copy-start.7
  5.5 0.7 %copy-done.7 = f32[2,128]{1,0:T(2,128)S(1)} copy-done((f32[2,128]{1,0:T(2,128)S(1)}, f32[2,128]{1,0:T(2,128)}, u32[]{:S(2)}) %copy-start.7) | copy-done | bytes 1048
  6.1 0.0 copy-start.9
  6.1 0.7 %copy-done.9 = f32[1,256]{1,0:T(1,128)S(1)} copy-done((f32[1,256]{1,0:T(1,128)S(1)}, f32[1,256]{1,0:T(1,128)}, u32[]{:S(2)}) %copy-start.9) | copy-done | bytes 1048
  6.8 44.4 %front.1 = (bf16[2,10,1024,128]{3,2,1,0:T(8,128)(2,1)}, f32[2,8,128]{2,1,0:T(8,128)S(1)}) custom-call(s32[1]{0:T(128)S(6)} %copy.11.t_ref, bf16[8,1024,128]{2,1,0:T(8,128)(2,1)S(1)} %bitcast.3, f32[1,256]{1,0:T(1,128)S(1)} %copy-done.9, bf16[512,256]{1,0:T(8,128)(2,1)S(1)} %copy-done.3, f32[2,128]{1,0:T(2,128)S(1)} %copy-done.5, f32[2,128]{1,0:T(2,128)S(1)} %copy-done.7, ...), custom_call_target="tpu_custom_call" | custom-call | tf_op jit(solution)/shard_map/front/pallas_call | solution.py:427
  51.2 0.0 copy-start.2
  51.2 1.0 %copy-done.2 = bf16[3,3,128,128]{3,2,1,0:T(8,128)(2,1)S(1)} copy-done((bf16[3,3,128,128]{3,2,1,0:T(8,128)(2,1)S(1)}, bf16[3,3,128,128]{3,2,1,0:T(8,128)(2,1)}, u32[]{:S(2)}) %copy-start.2) | copy-done | bytes 294936
  52.2 0.0 copy-start.4
  52.2 0.9 %copy-done.4 = bf16[3,128,128]{2,1,0:T(8,128)(2,1)S(1)} copy-done((bf16[3,128,128]{2,1,0:T(8,128)(2,1)S(1)}, bf16[3,128,128]{2,1,0:T(8,128)(2,1)}, u32[]{:S(2)}) %copy-start.4) | copy-done | bytes 98328
  53.1 0.0 copy-start.6
  53.1 0.7 %copy-done.6 = f32[2,128]{1,0:T(2,128)S(1)} copy-done((f32[2,128]{1,0:T(2,128)S(1)}, f32[2,128]{1,0:T(2,128)}, u32[]{:S(2)}) %copy-start.6) | copy-done | bytes 1048
  53.7 0.0 copy-start.8
  53.7 0.7 %copy-done.8 = f32[2,128]{1,0:T(2,128)S(1)} copy-done((f32[2,128]{1,0:T(2,128)S(1)}, f32[2,128]{1,0:T(2,128)}, u32[]{:S(2)}) %copy-start.8) | copy-done | bytes 1048
  54.4 11.3 %back.1 = (bf16[8,1024,128]{2,1,0:T(8,128)(2,1)}, f32[8,1024,128]{2,1,0:T(8,128)}) custom-call(s32[1]{0:T(128)S(6)} %copy.11.t_ref, bf16[2,10,1024,128]{3,2,1,0:T(8,128)(2,1)} %get-tuple-element.6.firsts_ref, f32[2,8,128]{2,1,0:T(8,128)S(1)} %get-tuple-element.7.stat_ref, bf16[8,1024,128]{2,1,0:T(8,128)(2,1)S(1)} %bitcast.4, f32[2,128]{1,0:T(2,128)S(1)} %copy-done.6, ...), custom_call_target="tpu_custom_call" | custom-call | tf_op jit(solution)/shard_map/back/pallas_call | solution.py:469
Async XLA Ops:
  1.3 1.6 %copy-start = (bf16[1,8,1024,128]{3,2,1,0:T(8,128)(2,1)S(1)}, bf16[1,8,1024,128]{3,2,1,0:T(8,128)(2,1)}, u32[]{:S(2)}) copy-start(bf16[1,8,1024,128]{3,2,1,0:T(8,128)(2,1)} %param.9) | copy-start | bytes 6291460
  2.9 1.0 %copy-start.1 = (bf16[3,3,128,128]{3,2,1,0:T(8,128)(2,1)S(1)}, bf16[3,3,128,128]{3,2,1,0:T(8,128)(2,1)}, u32[]{:S(2)}) copy-start(bf16[3,3,128,128]{3,2,1,0:T(8,128)(2,1)} %w_ref.2) | copy-start | bytes 884740
  3.8 0.9 %copy-start.3 = (bf16[512,256]{1,0:T(8,128)(2,1)S(1)}, bf16[512,256]{1,0:T(8,128)(2,1)}, u32[]{:S(2)}) copy-start(bf16[512,256]{1,0:T(8,128)(2,1)} %embed_ref.1) | copy-start | bytes 786436
  4.8 0.7 %copy-start.5 = (f32[2,128]{1,0:T(2,128)S(1)}, f32[2,128]{1,0:T(2,128)}, u32[]{:S(2)}) copy-start(f32[2,128]{1,0:T(2,128)} %gain_ref.3) | copy-start | bytes 3076
  5.5 0.7 %copy-start.7 = (f32[2,128]{1,0:T(2,128)S(1)}, f32[2,128]{1,0:T(2,128)}, u32[]{:S(2)}) copy-start(f32[2,128]{1,0:T(2,128)} %bias_ref.3) | copy-start | bytes 3076
  6.1 0.7 %copy-start.9 = (f32[1,256]{1,0:T(1,128)S(1)}, f32[1,256]{1,0:T(1,128)}, u32[]{:S(2)}) copy-start(f32[1,256]{1,0:T(1,128)} %constant.2.clone.freqs_ref) | copy-start | bytes 3076
  51.2 1.0 %copy-start.2 = (bf16[3,3,128,128]{3,2,1,0:T(8,128)(2,1)S(1)}, bf16[3,3,128,128]{3,2,1,0:T(8,128)(2,1)}, u32[]{:S(2)}) copy-start(bf16[3,3,128,128]{3,2,1,0:T(8,128)(2,1)} %w_ref.3) | copy-start | bytes 884740
  52.2 0.9 %copy-start.4 = (bf16[3,128,128]{2,1,0:T(8,128)(2,1)S(1)}, bf16[3,128,128]{2,1,0:T(8,128)(2,1)}, u32[]{:S(2)}) copy-start(bf16[3,128,128]{2,1,0:T(8,128)(2,1)} %tw_ref.1) | copy-start | bytes 294916
  53.1 0.7 %copy-start.6 = (f32[2,128]{1,0:T(2,128)S(1)}, f32[2,128]{1,0:T(2,128)}, u32[]{:S(2)}) copy-start(f32[2,128]{1,0:T(2,128)} %gain_ref.3) | copy-start | bytes 3076
  53.7 0.7 %copy-start.8 = (f32[2,128]{1,0:T(2,128)S(1)}, f32[2,128]{1,0:T(2,128)}, u32[]{:S(2)}) copy-start(f32[2,128]{1,0:T(2,128)} %bias_ref.3) | copy-start | bytes 3076

commit v2 on v1

--- a/solution.py
+++ b/solution.py
@@ -76,6 +76,19 @@
 
 def front(
     n,
+    t_hbm,
+    video_hbm,
+    freqs_hbm,
+    embed_hbm,
+    gain_hbm,
+    bias_hbm,
+    w_hbm,
+    tw_hbm,
+    w2_hbm,
+    firsts_ref,
+    factors,
+    wide2,
+    wtime,
     t_ref,
     video_ref,
     freqs_ref,
@@ -83,8 +96,9 @@
     gain_ref,
     bias_ref,
     w_ref,
-    firsts_ref,
-    stat_ref,
+    tw_ref,
+    w2_ref,
+    load_sem,
     halo,
     act,
     wide,
@@ -104,6 +118,8 @@
     core_rs,
     edge_ss,
     edge_rs,
+    relay_ss,
+    relay_rs,
     own_sem,
 ):
     height, width, channels = video_ref.shape
@@ -112,6 +128,24 @@
     r = lax.axis_index("rows")
     me = f * n + r
     barrier = pltpu.get_barrier_semaphore()
+    loads = [
+        pltpu.make_async_copy(src, dst, load_sem.at[i])
+        for i, (src, dst) in enumerate(
+            (
+                (video_hbm, video_ref),
+                (t_hbm, t_ref),
+                (freqs_hbm, freqs_ref),
+                (embed_hbm, embed_ref),
+                (gain_hbm, gain_ref),
+                (bias_hbm, bias_ref),
+                (w_hbm, w_ref),
+                (tw_hbm, tw_ref),
+                (w2_hbm, w2_ref),
+            )
+        )
+    ]
+    for load in loads:
+        load.start()
 
     def peer(d):
         q = lax.rem(me + d, 2 * n)
@@ -122,6 +156,30 @@
         _, device = peer(d)
         pl.semaphore_signal(barrier, 1, device_id=device, device_id_type=MESH)
 
+    pl.semaphore_wait(barrier, 2 * n - 1)
+
+    def halo_copy(side, target):
+        return pltpu.make_async_remote_copy(
+            video_hbm.at[height - 1 if side == 0 else 0],
+            halo.at[side],
+            halo_ss.at[side],
+            halo_rs.at[side],
+            device_id={"frames": f, "rows": target},
+            device_id_type=MESH,
+        )
+
+    has_low = r > 0
+    has_high = r < n - 1
+
+    @pl.when(has_high)
+    def _():
+        halo_copy(0, r + 1).start()
+
+    @pl.when(has_low)
+    def _():
+        halo_copy(1, r - 1).start()
+
+    loads[0].wait()
     sums[...] = jnp.zeros_like(sums)
 
     @pl.loop(0, height)
@@ -134,7 +192,6 @@
     s1_send[0:1] = jnp.sum(sums[0], axis=0, keepdims=True)
     s1_send[1:2] = jnp.sum(sums[1], axis=0, keepdims=True)
     s1_recv[r] = s1_send[...]
-    pl.semaphore_wait(barrier, 2 * n - 1)
 
     def s1_copy(src_row, dst_row):
         return pltpu.make_async_remote_copy(
@@ -150,28 +207,19 @@
     def _(d):
         s1_copy(r, lax.rem(r + d, n)).start()
 
-    def halo_copy(side, target):
-        return pltpu.make_async_remote_copy(
-            video_ref.at[height - 1 if side == 0 else 0],
-            halo.at[side],
-            halo_ss.at[side],
-            halo_rs.at[side],
-            device_id={"frames": f, "rows": target},
-            device_id_type=MESH,
-        )
-
-    has_low = r > 0
-    has_high = r < n - 1
-
-    @pl.when(has_high)
-    def _():
-        halo_copy(0, r + 1).start()
-
-    @pl.when(has_low)
-    def _():
-        halo_copy(1, r - 1).start()
-
+    for load in loads[1:]:
+        load.wait()
     put_weights(wide, w_ref)
+    put_weights(wide2, w2_ref)
+    wtime[0:channels] = tw_ref[1]
+    wtime[channels : 2 * channels] = tw_ref[2 - 2 * f]
+    step_now = jnp.full((8, channels), t_ref[0].astype(F32))
+    signal_now, noise_now = signal_noise(step_now)
+    signal_prev, noise_prev = signal_noise(step_now - STRIDE)
+    ratio = signal_prev / signal_now
+    factors[...] = jnp.zeros_like(factors)
+    factors[4:5] = ratio[0:1]
+    factors[5:6] = (noise_prev - ratio * noise_now)[0:1]
     angles = t_ref[0].astype(F32) * jnp.broadcast_to(freqs_ref[...], (16, freqs_ref.shape[1]))
     feats = jnp.concatenate([jnp.sin(angles), jnp.cos(angles)], axis=1).astype(BF16)
     film = jnp.dot(feats, embed_ref[...], preferred_element_type=F32)[0:1]
@@ -193,26 +241,6 @@
     @pl.loop(0, height)
     def _(h):
         activate(video_ref[h], h + 1)
-
-    zeros = jnp.zeros((width, 3 * channels), BF16)
-
-    @pl.when(has_low)
-    def _():
-        halo_copy(0, r - 1).wait_recv()
-        activate(halo[0], 0)
-
-    @pl.when(r == 0)
-    def _():
-        act[0] = zeros
-
-    @pl.when(has_high)
-    def _():
-        halo_copy(1, r + 1).wait_recv()
-        activate(halo[1], height + 1)
-
-    @pl.when(r == n - 1)
-    def _():
-        act[height + 1] = zeros
 
     def core_copy(p):
         return pltpu.make_async_remote_copy(
@@ -229,21 +257,31 @@
             first.at[pl.ds(2 * p, 2)], firsts_ref.at[0, pl.ds(1 + 2 * p, 2)], own_sem.at[p]
         )
 
-    def edge_copy(side, other, target):
+    def edge_copy(side, target):
         return pltpu.make_async_remote_copy(
             first.at[height - 1 if side == 0 else 0],
-            firsts_ref.at[other, 0 if side == 0 else height + 1],
-            edge_ss.at[side, other],
-            edge_rs.at[side, other],
-            device_id={"frames": 1 - f if other else f, "rows": target},
+            firsts_ref.at[0, 0 if side == 0 else height + 1],
+            edge_ss.at[side],
+            edge_rs.at[side],
+            device_id={"frames": f, "rows": target},
+            device_id_type=MESH,
+        )
+
+    def relay_copy(side):
+        row = 0 if side == 0 else height + 1
+        return pltpu.make_async_remote_copy(
+            firsts_ref.at[0, row],
+            firsts_ref.at[1, row],
+            relay_ss.at[side],
+            relay_rs.at[side],
+            device_id={"frames": 1 - f, "rows": r},
             device_id_type=MESH,
         )
 
     sums[...] = jnp.zeros_like(sums)
     step = width // 2
-    order = [0] + ([pairs - 1] if pairs > 1 else []) + list(range(1, pairs - 1))
-    for p in order:
-
+
+    def convolve(p):
         @pl.loop(0, width // step)
         def _(c):
             cols = pl.ds(pl.multiple_of(c * step, step), step)
@@ -257,19 +295,48 @@
 
         core_copy(p).start()
         own_copy(p).start()
-        if p == 0:
-
-            @pl.when(has_low)
-            def _():
-                edge_copy(1, 0, r - 1).start()
-                edge_copy(1, 1, r - 1).start()
-
-        if p == pairs - 1:
-
-            @pl.when(has_high)
-            def _():
-                edge_copy(0, 0, r + 1).start()
-                edge_copy(0, 1, r + 1).start()
+
+    for p in range(1, pairs - 1):
+        convolve(p)
+
+    zeros = jnp.zeros((width, 3 * channels), BF16)
+
+    @pl.when(has_low)
+    def _():
+        halo_copy(0, r - 1).wait_recv()
+        activate(halo[0], 0)
+
+    @pl.when(r == 0)
+    def _():
+        act[0] = zeros
+
+    if pairs > 1:
+        convolve(0)
+
+        @pl.when(has_low)
+        def _():
+            edge_copy(1, r - 1).start()
+
+    @pl.when(has_high)
+    def _():
+        halo_copy(1, r + 1).wait_recv()
+        activate(halo[1], height + 1)
+
+    @pl.when(r == n - 1)
+    def _():
+        act[height + 1] = zeros
+
+    convolve(pairs - 1)
+
+    @pl.when(has_high)
+    def _():
+        edge_copy(0, r + 1).start()
+
+    if pairs == 1:
+
+        @pl.when(has_low)
+        def _():
+            edge_copy(1, r - 1).start()
 
     s2_send[...] = jnp.zeros_like(s2_send)
     s2_send[0:1] = jnp.sum(sums[0], axis=0, keepdims=True)
@@ -296,8 +363,22 @@
         q, device = peer(d)
         s2_copy(q, q, device).wait_recv()
 
-    stat_ref[0] = jnp.sum(s2_recv[pl.ds(f * n, n)], axis=0)
-    stat_ref[1] = jnp.sum(s2_recv[pl.ds((1 - f) * n, n)], axis=0)
+    for i in range(2):
+        frame = f if i == 0 else 1 - f
+        stat = jnp.sum(s2_recv[pl.ds(frame * n, n)], axis=0)
+        a, b = half_factors(stat, count, gain_ref[1:2], bias_ref[1:2])
+        factors[2 * i : 2 * i + 1] = a
+        factors[2 * i + 1 : 2 * i + 2] = b
+
+    @pl.when(has_low)
+    def _():
+        edge_copy(0, r - 1).wait_recv()
+        relay_copy(0).start()
+
+    @pl.when(has_high)
+    def _():
+        edge_copy(1, r + 1).wait_recv()
+        relay_copy(1).start()
 
     for p in range(pairs):
         core_copy(p).wait()
@@ -306,16 +387,14 @@
     @pl.when(has_low)
     def _():
         halo_copy(1, r - 1).wait_send()
-        for other in range(2):
-            edge_copy(1, other, r - 1).wait_send()
-            edge_copy(0, other, r - 1).wait_recv()
+        edge_copy(1, r - 1).wait_send()
+        relay_copy(0).wait()
 
     @pl.when(has_high)
     def _():
         halo_copy(0, r + 1).wait_send()
-        for other in range(2):
-            edge_copy(0, other, r + 1).wait_send()
-            edge_copy(1, other, r + 1).wait_recv()
+        edge_copy(0, r + 1).wait_send()
+        relay_copy(1).wait()
 
     @pl.loop(1, n)
     def _(d):
@@ -328,45 +407,11 @@
 
 
 def back(
-    n,
-    t_ref,
-    firsts_ref,
-    stat_ref,
-    video_ref,
-    gain_ref,
-    bias_ref,
-    tw_ref,
-    w_ref,
-    next_ref,
-    pred_ref,
-    taps,
-    wide,
-    wtime,
-    factors,
-    *,
-    height,
+    n, firsts_ref, factors, video_ref, wtime, wide, next_ref, pred_ref, taps, *, height
 ):
     width, channels = firsts_ref.shape[2:]
     s = pl.program_id(0)
-    f = lax.axis_index("frames")
     r = lax.axis_index("rows")
-
-    @pl.when(s == 0)
-    def _():
-        put_weights(wide, w_ref)
-        wtime[0:channels] = tw_ref[1]
-        wtime[channels : 2 * channels] = tw_ref[2 - 2 * f]
-        count = float(height * n * width * (channels // GROUPS))
-        for i in range(2):
-            a, b = half_factors(stat_ref[i], count, gain_ref[1:2], bias_ref[1:2])
-            factors[2 * i : 2 * i + 1] = a
-            factors[2 * i + 1 : 2 * i + 2] = b
-        step_now = jnp.full((8, channels), t_ref[0].astype(F32))
-        signal_now, noise_now = signal_noise(step_now)
-        signal_prev, noise_prev = signal_noise(step_now - STRIDE)
-        ratio = signal_prev / signal_now
-        factors[4:5] = ratio[0:1]
-        factors[5:6] = (noise_prev - ratio * noise_now)[0:1]
 
     for j in range(2):
         row = 2 * s + j
@@ -421,18 +466,34 @@
         np.float32(-math.log(10000.0)) * np.arange(half, dtype=np.float32) / np.float32(half)
     )[None, :]
     vmem = pl.BlockSpec(memory_space=pltpu.VMEM)
-    smem = pl.BlockSpec(memory_space=pltpu.SMEM)
+    hbm = pl.BlockSpec(memory_space=pltpu.HBM)
     dma = pltpu.SemaphoreType.DMA
     pairs = height // 2
-    firsts, stat = pl.pallas_call(
+    args = (
+        timestep,
+        video,
+        jnp.asarray(freqs),
+        embed_weight,
+        norm_gain,
+        norm_bias,
+        conv_first,
+        temporal_weight,
+        conv_second,
+    )
+    firsts, factors, wide2, wtime = pl.pallas_call(
         functools.partial(front, n),
         out_shape=(
             jax.ShapeDtypeStruct((2, height + 2, width, channels), BF16),
-            jax.ShapeDtypeStruct((2, 8, channels), F32),
+            jax.ShapeDtypeStruct((8, channels), F32),
+            jax.ShapeDtypeStruct((12 * channels, 2 * channels), BF16),
+            jax.ShapeDtypeStruct((2 * channels, channels), BF16),
         ),
-        in_specs=[smem] + [vmem] * 6,
-        out_specs=(pl.BlockSpec(memory_space=pl.ANY), vmem),
+        in_specs=[hbm] * len(args),
+        out_specs=(hbm, vmem, vmem, vmem),
         scratch_shapes=[
+            pltpu.SMEM(timestep.shape, timestep.dtype),
+            *[pltpu.VMEM(x.shape, x.dtype) for x in args[1:]],
+            dma((len(args),)),
             pltpu.VMEM((2, width, channels), BF16),
             pltpu.VMEM((height + 2, width, 3 * channels), BF16),
             pltpu.VMEM((12 * channels, 2 * channels), BF16),
@@ -450,18 +511,17 @@
             dma((2 * n,)),
             dma((pairs,)),
             dma((pairs,)),
-            dma((2, 2)),
-            dma((2, 2)),
+            dma((2,)),
+            dma((2,)),
+            dma((2,)),
+            dma((2,)),
             dma((pairs,)),
         ],
         compiler_params=pltpu.CompilerParams(
-            collective_id=0, has_side_effects=True, vmem_limit_bytes=48 * 1024 * 1024
+            collective_id=0, has_side_effects=True, vmem_limit_bytes=60 * 1024 * 1024
         ),
         name="front",
-    )(timestep, video, jnp.asarray(freqs), embed_weight, norm_gain, norm_bias, conv_first)
-
-    def whole(*shape):
-        return pl.BlockSpec(shape, lambda s: (0,) * len(shape))
+    )(*args)
 
     def pair_block():
         return pl.BlockSpec((2, width, channels), lambda s: (jnp.maximum(s - 1, 0), 0, 0))
@@ -474,25 +534,19 @@
             jax.ShapeDtypeStruct((height, width, channels), F32),
         ),
         in_specs=[
-            smem,
             pl.BlockSpec((2, 2, width, channels), lambda s: (0, s, 0, 0)),
-            whole(2, 8, channels),
+            vmem,
             pair_block(),
-            whole(*norm_gain.shape),
-            whole(*norm_bias.shape),
-            whole(*temporal_weight.shape),
-            whole(*conv_second.shape),
+            vmem,
+            vmem,
         ],
         out_specs=(pair_block(), pair_block()),
         scratch_shapes=[
             pltpu.VMEM((height + 2, width, 3 * channels), BF16),
-            pltpu.VMEM((12 * channels, 2 * channels), BF16),
-            pltpu.VMEM((2 * channels, channels), BF16),
-            pltpu.VMEM((8, channels), F32),
         ],
-        compiler_params=pltpu.CompilerParams(vmem_limit_bytes=48 * 1024 * 1024),
+        compiler_params=pltpu.CompilerParams(vmem_limit_bytes=60 * 1024 * 1024),
         name="back",
-    )(timestep, firsts, stat, video, norm_gain, norm_bias, temporal_weight, conv_second)
+    )(firsts, factors, video, wtime, wide2)
     return next_video[None], predicted[None]
 
 

time: 66.2 us -> 54.4 us (0.82)
  local copies, waits for them, and re-layouts: 8.74 us -> 0 us
  Pallas kernels: 55.7 us -> 52.9 us
    unnamed x20 -> x0, local copies, waits for them, and re-layouts: 8.74 us -> none
    pallas_call x1, Pallas kernels: 44.4 us -> 41.5 us  [body(): pl.pallas_call(functools.partial(front, n), out_shape=(jax.ShapeDtypeStru...]
where the time goes in v2:
time: 54.4 us; the launch traced here: 54.2 us
  Pallas kernels  52.9 us (97%)
  between operations  1.29 us (2%)
    pallas_call x1, Pallas kernels, body(): pl.pallas_call(functools.partial(front, n), out_shape=(jax.ShapeDtypeStru...  41.5 us
    pallas_call x1, Pallas kernels, body(): pl.pallas_call(functools.partial(back, n, height=height), grid=(pairs + 1...  11.4 us

profile of v2, /device:TPU:9, one launch (start us, length us, event | category | flops | bytes accessed | tf_op | source)
XLA Modules:
  0.0 54.2 jit_solution(1292179274187149254)
XLA Ops:
  1.3 41.5 %front.1 = (bf16[2,10,1024,128]{3,2,1,0:T(8,128)(2,1)}, f32[8,128]{1,0:T(8,128)}, bf16[1536,256]{1,0:T(8,128)(2,1)}, bf16[256,128]{1,0:T(8,128)(2,1)}) custom-call(s32[1]{0:T(128)S(6)} %copy.11.t_hbm, bf16[8,1024,128]{2,1,0:T(8,128)(2,1)} %bitcast.3, f32[1,256]{1,0:T(1,128)} %constant.2.clone.freqs_hbm, bf16[512,256]{1,0:T(8,128)(2,1)} %embed_hbm.1, ...), custom_call_target="tpu_custom_call" | custom-call | tf_op jit(solution)/shard_map/front/pallas_call | solution.py:483
  42.8 11.4 %back.1 = (bf16[8,1024,128]{2,1,0:T(8,128)(2,1)}, f32[8,1024,128]{2,1,0:T(8,128)}) custom-call(bf16[2,10,1024,128]{3,2,1,0:T(8,128)(2,1)} %get-tuple-element.8.firsts_ref, f32[8,128]{1,0:T(8,128)} %get-tuple-element.9.factors, bf16[8,1024,128]{2,1,0:T(8,128)(2,1)} %bitcast.4, bf16[256,128]{1,0:T(8,128)(2,1)} %get-tuple-element.10.wtime, ...), custom_call_target="tpu_custom_call" | custom-call | tf_op jit(solution)/shard_map/back/pallas_call | solution.py:529

commit v3 on v2

--- a/solution.py
+++ b/solution.py
@@ -116,10 +116,6 @@
     s2_rs,
     core_ss,
     core_rs,
-    edge_ss,
-    edge_rs,
-    relay_ss,
-    relay_rs,
     own_sem,
 ):
     height, width, channels = video_ref.shape
@@ -158,12 +154,12 @@
 
     pl.semaphore_wait(barrier, 2 * n - 1)
 
-    def halo_copy(side, target):
+    def halo_copy(side, target, k):
         return pltpu.make_async_remote_copy(
-            video_hbm.at[height - 1 if side == 0 else 0],
-            halo.at[side],
-            halo_ss.at[side],
-            halo_rs.at[side],
+            video_hbm.at[height - 1 - k if side == 0 else k],
+            halo.at[side, k],
+            halo_ss.at[side, k],
+            halo_rs.at[side, k],
             device_id={"frames": f, "rows": target},
             device_id_type=MESH,
         )
@@ -173,11 +169,11 @@
 
     @pl.when(has_high)
     def _():
-        halo_copy(0, r + 1).start()
+        halo_copy(0, r + 1, 0).start()
 
     @pl.when(has_low)
     def _():
-        halo_copy(1, r - 1).start()
+        halo_copy(1, r - 1, 0).start()
 
     loads[0].wait()
     sums[...] = jnp.zeros_like(sums)
@@ -231,6 +227,14 @@
         q = lax.rem(r + d, n)
         s1_copy(q, q).wait_recv()
 
+    @pl.when(has_high)
+    def _():
+        halo_copy(0, r + 1, 1).start()
+
+    @pl.when(has_low)
+    def _():
+        halo_copy(1, r - 1, 1).start()
+
     count = float(height * n * width * (channels // GROUPS))
     a, b = half_factors(jnp.sum(s1_recv[...], axis=0), count, gain_ref[0:1], bias_ref[0:1])
 
@@ -240,11 +244,11 @@
 
     @pl.loop(0, height)
     def _(h):
-        activate(video_ref[h], h + 1)
+        activate(video_ref[h], h + 2)
 
     def core_copy(p):
         return pltpu.make_async_remote_copy(
-            first.at[pl.ds(2 * p, 2)],
+            first.at[pl.ds(1 + 2 * p, 2)],
             firsts_ref.at[1, pl.ds(1 + 2 * p, 2)],
             core_ss.at[p],
             core_rs.at[p],
@@ -254,28 +258,23 @@
 
     def own_copy(p):
         return pltpu.make_async_copy(
-            first.at[pl.ds(2 * p, 2)], firsts_ref.at[0, pl.ds(1 + 2 * p, 2)], own_sem.at[p]
-        )
-
-    def edge_copy(side, target):
-        return pltpu.make_async_remote_copy(
-            first.at[height - 1 if side == 0 else 0],
-            firsts_ref.at[0, 0 if side == 0 else height + 1],
-            edge_ss.at[side],
-            edge_rs.at[side],
-            device_id={"frames": f, "rows": target},
-            device_id_type=MESH,
-        )
-
-    def relay_copy(side):
+            first.at[pl.ds(1 + 2 * p, 2)], firsts_ref.at[0, pl.ds(1 + 2 * p, 2)], own_sem.at[p]
+        )
+
+    def edge_copies(side):
         row = 0 if side == 0 else height + 1
-        return pltpu.make_async_remote_copy(
-            firsts_ref.at[0, row],
-            firsts_ref.at[1, row],
-            relay_ss.at[side],
-            relay_rs.at[side],
-            device_id={"frames": 1 - f, "rows": r},
-            device_id_type=MESH,
+        return (
+            pltpu.make_async_remote_copy(
+                first.at[row],
+                firsts_ref.at[1, row],
+                core_ss.at[pairs + side],
+                core_rs.at[pairs + side],
+                device_id={"frames": 1 - f, "rows": r},
+                device_id_type=MESH,
+            ),
+            pltpu.make_async_copy(
+                first.at[row], firsts_ref.at[0, row], own_sem.at[pairs + side]
+            ),
         )
 
     sums[...] = jnp.zeros_like(sums)
@@ -285,10 +284,10 @@
         @pl.loop(0, width // step)
         def _(c):
             cols = pl.ds(pl.multiple_of(c * step, step), step)
-            acc = pair_dot(act, 2 * p, cols, wide)
+            acc = pair_dot(act, 2 * p + 1, cols, wide)
             for o in range(2):
                 out = (acc[:, o * channels : (o + 1) * channels] * scale + shift).astype(BF16)
-                first[2 * p + o, cols, :] = out
+                first[1 + 2 * p + o, cols, :] = out
                 value = out.astype(F32)
                 sums[0] += fold8(value)
                 sums[1] += fold8(value * value)
@@ -303,40 +302,26 @@
 
     @pl.when(has_low)
     def _():
-        halo_copy(0, r - 1).wait_recv()
-        activate(halo[0], 0)
+        halo_copy(0, r - 1, 0).wait_recv()
+        activate(halo[0, 0], 1)
 
     @pl.when(r == 0)
     def _():
-        act[0] = zeros
+        act[1] = zeros
 
     if pairs > 1:
         convolve(0)
 
-        @pl.when(has_low)
-        def _():
-            edge_copy(1, r - 1).start()
-
     @pl.when(has_high)
     def _():
-        halo_copy(1, r + 1).wait_recv()
-        activate(halo[1], height + 1)
+        halo_copy(1, r + 1, 0).wait_recv()
+        activate(halo[1, 0], height + 2)
 
     @pl.when(r == n - 1)
     def _():
-        act[height + 1] = zeros
+        act[height + 2] = zeros
 
     convolve(pairs - 1)
-
-    @pl.when(has_high)
-    def _():
-        edge_copy(0, r + 1).start()
-
-    if pairs == 1:
-
-        @pl.when(has_low)
-        def _():
-            edge_copy(1, r - 1).start()
 
     s2_send[...] = jnp.zeros_like(s2_send)
     s2_send[0:1] = jnp.sum(sums[0], axis=0, keepdims=True)
@@ -358,6 +343,31 @@
         q, device = peer(d)
         s2_copy(me, q, device).start()
 
+    def beyond(side):
+        base = 0 if side == 0 else height
+        row = 0 if side == 0 else height + 1
+
+        @pl.loop(0, width // step)
+        def _(c):
+            cols = pl.ds(pl.multiple_of(c * step, step), step)
+            acc = pair_dot(act, base, cols, wide)[:, side * channels : (side + 1) * channels]
+            first[row, cols, :] = (acc * scale + shift).astype(BF16)
+
+        for copy in edge_copies(side):
+            copy.start()
+
+    @pl.when(has_low)
+    def _():
+        halo_copy(0, r - 1, 1).wait_recv()
+        activate(halo[0, 1], 0)
+        beyond(0)
+
+    @pl.when(has_high)
+    def _():
+        halo_copy(1, r + 1, 1).wait_recv()
+        activate(halo[1, 1], height + 3)
+        beyond(1)
+
     @pl.loop(1, 2 * n)
     def _(d):
         q, device = peer(d)
@@ -370,31 +380,23 @@
         factors[2 * i : 2 * i + 1] = a
         factors[2 * i + 1 : 2 * i + 2] = b
 
-    @pl.when(has_low)
-    def _():
-        edge_copy(0, r - 1).wait_recv()
-        relay_copy(0).start()
-
-    @pl.when(has_high)
-    def _():
-        edge_copy(1, r + 1).wait_recv()
-        relay_copy(1).start()
-
     for p in range(pairs):
         core_copy(p).wait()
         own_copy(p).wait()
 
     @pl.when(has_low)
     def _():
-        halo_copy(1, r - 1).wait_send()
-        edge_copy(1, r - 1).wait_send()
-        relay_copy(0).wait()
+        for k in range(2):
+            halo_copy(1, r - 1, k).wait_send()
+        for copy in edge_copies(0):
+            copy.wait()
 
     @pl.when(has_high)
     def _():
-        halo_copy(0, r + 1).wait_send()
-        edge_copy(0, r + 1).wait_send()
-        relay_copy(1).wait()
+        for k in range(2):
+            halo_copy(0, r + 1, k).wait_send()
+        for copy in edge_copies(1):
+            copy.wait()
 
     @pl.loop(1, n)
     def _(d):
@@ -494,28 +496,24 @@
             pltpu.SMEM(timestep.shape, timestep.dtype),
             *[pltpu.VMEM(x.shape, x.dtype) for x in args[1:]],
             dma((len(args),)),
-            pltpu.VMEM((2, width, channels), BF16),
-            pltpu.VMEM((height + 2, width, 3 * channels), BF16),
+            pltpu.VMEM((2, 2, width, channels), BF16),
+            pltpu.VMEM((height + 4, width, 3 * channels), BF16),
             pltpu.VMEM((12 * channels, 2 * channels), BF16),
-            pltpu.VMEM((height, width, channels), BF16),
+            pltpu.VMEM((height + 2, width, channels), BF16),
             pltpu.VMEM((8, channels), F32),
             pltpu.VMEM((n, 8, channels), F32),
             pltpu.VMEM((8, channels), F32),
             pltpu.VMEM((2 * n, 8, channels), F32),
             pltpu.VMEM((2, 8, channels), F32),
-            dma((2,)),
-            dma((2,)),
+            dma((2, 2)),
+            dma((2, 2)),
             dma((n,)),
             dma((n,)),
             dma((2 * n,)),
             dma((2 * n,)),
-            dma((pairs,)),
-            dma((pairs,)),
-            dma((2,)),
-            dma((2,)),
-            dma((2,)),
-            dma((2,)),
-            dma((pairs,)),
+            dma((pairs + 2,)),
+            dma((pairs + 2,)),
+            dma((pairs + 2,)),
         ],
         compiler_params=pltpu.CompilerParams(
             collective_id=0, has_side_effects=True, vmem_limit_bytes=60 * 1024 * 1024

time: 54.4 us -> 49.3 us (0.906)
  Pallas kernels: 52.9 us -> 47.8 us
    pallas_call x1, Pallas kernels: 41.5 us -> 36.4 us  [body(): pl.pallas_call(functools.partial(front, n), out_shape=(jax.ShapeDtypeStru...]
where the time goes in v3:
time: 49.3 us; the launch traced here: 49.1 us
  Pallas kernels  47.8 us (97%)
  between operations  1.29 us (3%)
    pallas_call x1, Pallas kernels, body(): pl.pallas_call(functools.partial(front, n), out_shape=(jax.ShapeDtypeStru...  36.4 us
    pallas_call x1, Pallas kernels, body(): pl.pallas_call(functools.partial(back, n, height=height), grid=(pairs + 1...  11.4 us

profile of v3, /device:TPU:9, one launch (start us, length us, event | category | flops | bytes accessed | tf_op | source)
XLA Modules:
  0.0 49.1 jit_solution(7193371457595610194)
XLA Ops:
  1.3 36.4 %front.1 = (bf16[2,10,1024,128]{3,2,1,0:T(8,128)(2,1)}, f32[8,128]{1,0:T(8,128)}, bf16[1536,256]{1,0:T(8,128)(2,1)}, bf16[256,128]{1,0:T(8,128)(2,1)}) custom-call(s32[1]{0:T(128)S(6)} %copy.11.t_hbm, bf16[8,1024,128]{2,1,0:T(8,128)(2,1)} %bitcast.3, f32[1,256]{1,0:T(1,128)} %constant.2.clone.freqs_hbm, bf16[512,256]{1,0:T(8,128)(2,1)} %embed_hbm.1, ...), custom_call_target="tpu_custom_call" | custom-call | tf_op jit(solution)/shard_map/front/pallas_call | solution.py:485
  37.7 11.4 %back.1 = (bf16[8,1024,128]{2,1,0:T(8,128)(2,1)}, f32[8,1024,128]{2,1,0:T(8,128)}) custom-call(bf16[2,10,1024,128]{3,2,1,0:T(8,128)(2,1)} %get-tuple-element.8.firsts_ref, f32[8,128]{1,0:T(8,128)} %get-tuple-element.9.factors, bf16[8,1024,128]{2,1,0:T(8,128)(2,1)} %bitcast.4, bf16[256,128]{1,0:T(8,128)(2,1)} %get-tuple-element.10.wtime, ...), custom_call_target="tpu_custom_call" | custom-call | tf_op jit(solution)/shard_map/back/pallas_call | solution.py:527

commit v4 on v3

--- a/solution.py
+++ b/solution.py
@@ -278,7 +278,7 @@
         )
 
     sums[...] = jnp.zeros_like(sums)
-    step = width // 2
+    step = width
 
     def convolve(p):
         @pl.loop(0, width // step)
@@ -433,7 +433,7 @@
 
     @pl.when(s > 0)
     def _():
-        step = width // 2
+        step = width
 
         @pl.loop(0, width // step)
         def _(c):

time: 49.3 us -> 48.3 us (0.980)
  Pallas kernels: 47.8 us -> 46.8 us
    pallas_call x1, Pallas kernels: 11.4 us -> 10.8 us  [body(): pl.pallas_call(functools.partial(back, n, height=height), grid=(pairs + 1...]
where the time goes in v4:
time: 48.3 us; the launch traced here: 48.1 us
  Pallas kernels  46.8 us (97%)
  between operations  1.29 us (3%)
    pallas_call x1, Pallas kernels, body(): pl.pallas_call(functools.partial(front, n), out_shape=(jax.ShapeDtypeStru...  36 us
    pallas_call x1, Pallas kernels, body(): pl.pallas_call(functools.partial(back, n, height=height), grid=(pairs + 1...  10.8 us

profile of v4, /device:TPU:9, one launch (start us, length us, event | category | flops | bytes accessed | tf_op | source)
XLA Modules:
  0.0 48.1 jit_solution(10425077485970540890)
XLA Ops:
  1.3 36.0 %front.1 = (bf16[2,10,1024,128]{3,2,1,0:T(8,128)(2,1)}, f32[8,128]{1,0:T(8,128)}, bf16[1536,256]{1,0:T(8,128)(2,1)}, bf16[256,128]{1,0:T(8,128)(2,1)}) custom-call(s32[1]{0:T(128)S(6)} %copy.11.t_hbm, bf16[8,1024,128]{2,1,0:T(8,128)(2,1)} %bitcast.3, f32[1,256]{1,0:T(1,128)} %constant.2.clone.freqs_hbm, bf16[512,256]{1,0:T(8,128)(2,1)} %embed_hbm.1, ...), custom_call_target="tpu_custom_call" | custom-call | tf_op jit(solution)/shard_map/front/pallas_call | solution.py:485
  37.3 10.8 %back.1 = (bf16[8,1024,128]{2,1,0:T(8,128)(2,1)}, f32[8,1024,128]{2,1,0:T(8,128)}) custom-call(bf16[2,10,1024,128]{3,2,1,0:T(8,128)(2,1)} %get-tuple-element.8.firsts_ref, f32[8,128]{1,0:T(8,128)} %get-tuple-element.9.factors, bf16[8,1024,128]{2,1,0:T(8,128)(2,1)} %bitcast.4, bf16[256,128]{1,0:T(8,128)(2,1)} %get-tuple-element.10.wtime, ...), custom_call_target="tpu_custom_call" | custom-call | tf_op jit(solution)/shard_map/back/pallas_call | solution.py:527
